TPU v7x, 32 devices: a whole 2x2x4 slice. The times are simulated.
32 devices in a mesh: dp: 4 (over y, x), shard: 8 (over z, core).
Axes of the slice: x: 2, y: 2, z: 4, core: 2. Of those that a mesh axis runs over, the one named last changes fastest.
Arguments:
- stats_partial: float32 [4, 8, 2, 512, 512], P('dp', None, None, 'shard'), may hold values from -800 to 800, as said below
- gradient: bfloat16 [8, 512, 512], P(None, 'shard'), may hold values from -240 to 240
- owner_of: int32 [8], replicated, may hold values from 0 to 7, as said below
- layer_count: int32 [4], replicated, may hold values from 1 to 4, 8 in all
Outputs:
- preconditioned: bfloat16 [8, 2, 512, 512], P('shard', None, 'dp')
Inputs may be any that keep to these rules, and one draw needn't show every extreme that they name: `owner_of`: each owner holds 0 to 2 blocks, and in every draw some owner holds exactly 2. `layer_count`: the counts sum to 8. `stats_partial`: each [512, 512] slice is symmetric positive definite.
All inputs are finite; a program needn't handle non-finite values.
Results may differ from a plain program's by a relative error of at most 0.0062.
The roundings to bfloat16 on the way count: a program that leaves them out, or rounds other values in their place, can miss the bound.
Values may be sent and summed in bfloat16 or wider, within the bound.
A program may use at most 64 MiB of HBM per device.

v0:
```python
import jax
import jax.numpy as jnp
from jax import lax
from jax.sharding import PartitionSpec as P

B = 512
ITERS = 3
OCAP = 2
LAYERS = 4


highest = lax.Precision.HIGHEST


def product(left_side, right_side):
    return jnp.dot(left_side, right_side, precision=highest, preferred_element_type=jnp.float32)


def inverse_root(statistic):
    identity = jnp.eye(B, dtype=jnp.float32)
    magnitude = B * jnp.sqrt(jnp.mean(statistic * statistic) + 1e-06)
    matrix = statistic / magnitude
    factor = identity * magnitude ** (-0.25)
    for number in range(ITERS):
        update = (5.0 * identity - matrix) * 0.25
        factor = product(factor, update)
        if number + 1 < ITERS:
            square = product(update, update)
            fourth = product(square, square)
            matrix = product(fourth, matrix)
    return factor.astype(jnp.bfloat16)


def precondition(left_all, right_all, grad_full, member, quarter):
    left_rows = lax.dynamic_slice_in_dim(left_all, member * quarter, quarter, 1)
    middle = jnp.einsum(
        "kqb,kbc->kqc", left_rows, grad_full, preferred_element_type=jnp.float32
    ).astype(jnp.bfloat16)
    result = jnp.einsum("kqc,kcd->kqd", middle, right_all, preferred_element_type=jnp.float32)
    grad_rows = lax.dynamic_slice_in_dim(grad_full, member * quarter, quarter, 1).astype(
        jnp.float32
    )
    return (
        result,
        jnp.sum(grad_rows * grad_rows, axis=(1, 2)),
        jnp.sum(result * result, axis=(1, 2)),
    )


def on_device(stats_partial, gradient, owner_of, layer_count):
    shards = lax.axis_size("shard")
    groups = lax.axis_size("dp")
    my_shard = lax.axis_index("shard")
    member = lax.axis_index("dp")
    blocks = owner_of.shape[0]
    quarter = B // groups
    block_ids = jnp.arange(blocks, dtype=jnp.int32)
    same_owner = (owner_of[:, None] == owner_of[None, :]) & (
        block_ids[None, :] < block_ids[:, None]
    )
    earlier = jnp.sum(same_owner.astype(jnp.int32), axis=1)
    target = owner_of * OCAP + earlier
    places = jnp.arange(shards * OCAP, dtype=jnp.int32)
    matches = target[:, None] == places[None, :]
    filled = jnp.any(matches, axis=0)
    chosen = jnp.sum(jnp.where(matches, block_ids[:, None], 0), axis=0)
    all_places = (
        jnp.arange(OCAP, dtype=jnp.int32)[:, None]
        + OCAP * jnp.arange(shards, dtype=jnp.int32)[None, :]
    )
    grad_pick = jnp.take(chosen, all_places)
    grad_live = jnp.take(filled, all_places)
    layer_ends = jnp.cumsum(layer_count)
    layer_of = jnp.sum((block_ids[:, None] >= layer_ends[None, :]).astype(jnp.int32), axis=1)
    local = stats_partial[0]
    local_rows = local.shape[2]
    slot_index = member // 2
    members = jnp.arange(groups, dtype=jnp.int32)
    place_all = jnp.arange(shards, dtype=jnp.int32)[None, :] * OCAP + (members // 2)[:, None]
    pick_all = jnp.take(chosen, place_all)
    live_all = jnp.take(filled, place_all)
    flat_local = local.reshape(blocks * 2, local_rows, B)
    laid = jnp.where(
        live_all[:, :, None, None],
        jnp.take(flat_local, pick_all * 2 + (members % 2)[:, None], axis=0),
        0.0,
    )
    outgoing = lax.psum_scatter(laid, "dp", scatter_dimension=0, tiled=True)[0]
    incoming = lax.all_to_all(outgoing, "shard", split_axis=0, concat_axis=0, tiled=True)
    statistic = incoming.reshape(B, B)
    my_blocks = jnp.take(chosen, my_shard * OCAP + jnp.arange(OCAP, dtype=jnp.int32))
    mine_live = jnp.take(filled, my_shard * OCAP + slot_index)
    statistic = jnp.where(mine_live, statistic, jnp.eye(B, dtype=jnp.float32))
    factor = inverse_root(statistic)
    factors = lax.all_gather(factor[None], "dp", axis=0, tiled=True).reshape(OCAP, 2, B, B)
    grad_send = jnp.where(
        grad_live[:, :, None, None],
        jnp.take(gradient, grad_pick, axis=0),
        jnp.zeros((), jnp.bfloat16),
    )
    grad_full = lax.all_to_all(grad_send, "shard", split_axis=1, concat_axis=1, tiled=True).reshape(
        OCAP, B, B
    )
    result, grad_terms, result_terms = precondition(
        factors[:, 0], factors[:, 1], grad_full, member, quarter
    )
    layer_hot = (
        jnp.take(layer_of, my_blocks)[:, None] == jnp.arange(LAYERS, dtype=jnp.int32)[None, :]
    ).astype(jnp.float32)
    grad_total, result_total = lax.psum(
        (
            jnp.sum(layer_hot * grad_terms[:, None], axis=0),
            jnp.sum(layer_hot * result_terms[:, None], axis=0),
        ),
        ("dp", "shard"),
    )
    graft_ratio = jnp.sqrt((grad_total + 1e-06) / (result_total + 1e-06))
    scaled = (result * jnp.sum(layer_hot * graft_ratio[None, :], axis=1)[:, None, None]).astype(
        jnp.bfloat16
    )
    return scaled[None]


def solution(mesh):
    placed = (P("dp", None, None, "shard", None), P(None, "shard", None), P(), P())
    return jax.shard_map(
        on_device,
        mesh=mesh,
        in_specs=placed,
        out_specs=P("shard", None, "dp", None),
        check_vma=False,
    )
```

profile of v0, /device:TPU:0, one launch (start us, length us, event | category | flops | bytes accessed | tf_op | source)
XLA Modules:
  0.0 213.3 jit_solution(4676955721847245528)
XLA Ops:
  6.5 0.0 copy-start
  6.5 0.0 reduce-scatter.4.cloned.1.call-start
  6.5 1.0 convert_reduce_fusion
  7.5 0.7 multiply_add_fusion.1
  8.2 0.1 select_reduce_fusion
  8.3 0.1 fusion.27
  8.4 0.1 compare_select_fusion.2
  8.5 0.1 reshape.530
  8.6 0.7 gather_fusion.1
  9.2 0.1 gather.45
  9.3 0.1 reshape.537
  9.4 0.1 compare_select_fusion
  9.5 0.1 reshape.546
  9.6 0.7 gather_fusion
  10.3 0.1 reshape.529
  10.4 0.0 copy-done
  10.4 2.8 %gather_fusion.2 = f32[32,64,512]{2,1,0:T(8,128)} fusion(f32[16,64,512]{2,1,0:T(8,128)S(1)} %bitcast.61, s32[1024]{0:T(1024)S(1)} %pad_clamp_fusion.4), kind=kCustom, calls=%fused_computation.2 | custom fusion | bytes 8388736 | tf_op jit(solution)/shard_map/jit(_take)/gather | solution.py:85
  13.2 0.1 broadcast_select_fusion.1
  13.3 5.1 %select_select_fusion = f32[4,8,64,512]{3,2,1,0:T(8,128)} fusion(f32[4,8,64,512]{3,2,1,0:T(8,128)} %bitcast.62, pred[4,8]{1,0:T(4,128)(4,1)S(1)} %get-tuple-element.21, pred[4,8]{1,0:T(4,128)(4,1)S(1)} %get-tuple-element.20), kind=kLoop, calls=%fused_computation.8 | loop fusion | flops 2097152 | bytes 8388672 | tf_op jit(solution)/shard_map/jit(_where)/select_n | solution.py:83
  18.4 0.0 reduce-scatter.4.cloned.1.call-update
  18.4 55.6 %reduce-scatter.4.cloned.1.call-done = f32[1,8,64,512]{3,2,1,0:T(8,128)} async-done(((f32[4,8,64,512]{3,2,1,0:T(8,128)}), f32[1,8,64,512]{3,2,1,0:T(8,128)}) %reduce-scatter.4.cloned.1.call-update) | async-done | bytes 1048592
  74.0 4.6 %all-to-all-start = ((f32[8,64,512]{2,1,0:T(8,128)}), f32[8,64,512]{2,1,0:T(8,128)S(1)}, u32[]{:S(2)}, u32[]{:S(2)}) async-start(f32[8,64,512]{2,1,0:T(8,128)} %bitcast.69), calls=%async_computation | async-start | bytes 2097152 | tf_op jit(solution)/shard_map/all_to_all | solution.py:89
  78.6 0.0 all-gather.3.cloned.1.call-start
  78.6 0.7 dynamic-slice.3
  80.0 25.2 %all-to-all-done = f32[8,64,512]{2,1,0:T(8,128)S(1)} async-done(((f32[8,64,512]{2,1,0:T(8,128)}), f32[8,64,512]{2,1,0:T(8,128)S(1)}, u32[]{:S(2)}, u32[]{:S(2)}) %all-to-all-start) | async-done | bytes 1048608 | tf_op jit(solution)/shard_map/all_to_all | solution.py:89
  105.2 1.2 multiply_reduce_fusion
  107.1 0.3 subtract_multiply_fusion
  107.4 1.8 fusion.48
  109.3 1.8 fusion.49
  111.1 0.1 fusion.6
  111.3 1.9 fusion.3
  113.1 1.9 fusion.50
  115.0 1.9 fusion.8
  116.9 1.9 fusion.10
  118.8 2.0 fusion.51
  120.9 1.9 fusion
  122.7 2.6 %convolution_convert_fusion = bf16[512,512]{1,0:T(8,128)(2,1)} fusion(f32[512,512]{1,0:T(8,128)S(1)} %fusion.10, f32[512,512]{1,0:T(8,128)S(1)} %fusion), kind=kOutput, calls=%fused_computation.13 | convolution fusion | flops 1610874880 | bytes 2621440 | tf_op jit(solution)/shard_map/dot_general | solution.py:16
  125.4 0.0 all-gather.3.cloned.1.call-update
  125.4 0.1 reshape.554
  125.5 0.7 gather_fusion.4
  126.2 0.7 gather_fusion.3
  126.8 0.1 gather.49
  126.9 0.1 reshape.561
  127.0 0.1 reshape.570
  127.1 0.1 reshape.553
  127.2 0.0 copy-start.1
  127.2 1.7 gather_fusion.5
  128.9 0.2 select_select_fusion.1
  129.1 1.1 copy.14
  130.2 4.2 %all-to-all-start.1 = ((bf16[2,8,64,512]{3,2,0,1:T(8,128)(2,1)}), bf16[2,8,64,512]{3,2,0,1:T(8,128)(2,1)}, u32[]{:S(2)}, u32[]{:S(2)}) async-start(bf16[2,8,64,512]{3,2,0,1:T(8,128)(2,1)} %copy.14), calls=%async_computation.1 | async-start | bytes 2097152 | tf_op jit(solution)/shard_map/all_to_all | solution.py:101
  134.4 0.0 copy-done.1
  134.4 0.2 reduce-window.8
  134.6 0.6 gather_fusion.6
  135.3 0.1 convert_reduce_fusion.1
  135.4 0.6 gather_fusion.7
  136.0 25.0 %all-to-all-done.1 = bf16[2,8,64,512]{3,2,0,1:T(8,128)(2,1)} async-done(((bf16[2,8,64,512]{3,2,0,1:T(8,128)(2,1)}), bf16[2,8,64,512]{3,2,0,1:T(8,128)(2,1)}, u32[]{:S(2)}, u32[]{:S(2)}) %all-to-all-start.1) | async-done | bytes 1048608 | tf_op jit(solution)/shard_map/all_to_all | solution.py:101
  161.0 1.3 copy.15
  162.3 0.2 multiply_reduce_fusion.2
  162.5 2.3 %slice.29 = bf16[2,1,512,512]{3,2,1,0:T(8,128)(2,1)} slice(bf16[2,2,512,512]{3,2,1,0:T(8,128)(2,1)} %bitcast.67), slice={[0:2], [0:1], [0:512], [0:512]} | slice | bytes 2097152 | tf_op jit(solution)/shard_map/slice | solution.py:105
  164.8 2.6 %multiply_reduce_fusion.1 = (f32[2]{0:T(128)S(1)}, f32[2,128,512]{2,1,0:T(8,128)}) fusion(bf16[2,2,512,512]{3,2,1,0:T(8,128)(2,1)} %bitcast.68, bf16[2,512,512]{2,1,0:T(8,128)(2,1)S(1)} %bitcast.65, bf16[2,1,512,512]{3,2,1,0:T(8,128)(2,1)} %slice.29, s32[]{:T(128)S(6)} %select_n.313), kind=kOutput, calls=%fused_computation.32 | convolution fusion | flops 268828672 | bytes 2883596 | tf_op jit(solution)/shard_map/kqc,kcd->kqd/dot_general | solution.py:39
  167.4 0.1 select_reduce_fusion.3
  167.5 36.9 %all-reduce.1 = (f32[4]{0:T(128)S(1)}, f32[4]{0:T(128)S(1)}) all-reduce(f32[4]{0:T(128)S(1)} %get-tuple-element.17, f32[4]{0:T(128)S(1)} %get-tuple-element.16), channel_id=1, replica_groups=mesh['dp'=4,'shard'=8] {'dp','shard'}, use_global_device_ids=true, to_apply=%region_12.13 | all-reduce | flops 8 | bytes 64 | tf_op jit(solution)/shard_map/psum | solution.py:110
  204.4 0.2 select_reduce_fusion.1
  204.6 1.9 fusion.22
  (17 shorter events, 0.1 us)
Async XLA Ops:
  6.5 3.9 %copy-start = (f32[1,8,2,64,512]{4,3,2,1,0:T(8,128)S(1)}, f32[1,8,2,64,512]{4,3,2,1,0:T(8,128)}, u32[]{:S(2)}) copy-start(f32[1,8,2,64,512]{4,3,2,1,0:T(8,128)} %param.4) | copy-start | bytes 6291460
  6.5 67.4 %reduce-scatter.4.cloned.1.call-start = ((), (), s32[]{:S(2)}) async-start(), calls=%async_computation.4 | async-start | bytes 5242880
  74.0 31.2 %all-to-all-start = ((f32[8,64,512]{2,1,0:T(8,128)}), f32[8,64,512]{2,1,0:T(8,128)S(1)}, u32[]{:S(2)}, u32[]{:S(2)}) async-start(f32[8,64,512]{2,1,0:T(8,128)} %bitcast.69), calls=%async_computation | async-start | bytes 2097152 | tf_op jit(solution)/shard_map/all_to_all | solution.py:89
  78.6 84.0 %all-gather.3.cloned.1.call-start = ((), (), s32[]{:S(2)}) async-start(), calls=%async_computation.3 | async-start | bytes 2621440 | tf_op jit(solution)/shard_map/all_gather | solution.py:95
  127.2 7.2 %copy-start.1 = (s32[4]{0:T(128)S(1)}, s32[4]{0:T(128)}, u32[]{:S(2)}) copy-start(s32[4]{0:T(128)} %param.7) | copy-start | bytes 52
  130.2 30.8 %all-to-all-start.1 = ((bf16[2,8,64,512]{3,2,0,1:T(8,128)(2,1)}), bf16[2,8,64,512]{3,2,0,1:T(8,128)(2,1)}, u32[]{:S(2)}, u32[]{:S(2)}) async-start(bf16[2,8,64,512]{3,2,0,1:T(8,128)(2,1)} %copy.14), calls=%async_computation.1 | async-start | bytes 2097152 | tf_op jit(solution)/shard_map/all_to_all | solution.py:101
Sparse Core Ops, SparseCore 0:
  18.5 55.3 reduce-scatter.3
  125.5 33.2 all-gather.2
where the time goes:
time: 214 us; the launch traced here: 213 us
  waiting for transfers between devices  106 us (50%)
  blocking collectives  36.9 us (17%)
  matrix products  20.4 us (10%)
  between operations  15.1 us (7%)
  local copies, waits for them, and re-layouts  14.6 us (7%)
  other arithmetic  11.7 us (5%)
  starting transfers between devices  8.9 us (4%)
    unnamed x3, waiting for transfers between devices  55.6 us
    psum x1, blocking collectives, on_device(): lax.psum((jnp.sum(layer_hot * grad_terms[:, None], axis=0), jnp.sum(layer...  36.9 us
    all_to_all x1, waiting for transfers between devices, on_device(): lax.all_to_all(outgoing, 'shard', split_axis=0, concat_axis=0, tiled=True)  25.2 us
    all_to_all x1, waiting for transfers between devices, on_device(): lax.all_to_all(grad_send, 'shard', split_axis=1, concat_axis=1, tiled=True)  25 us
    dot_general x9, matrix products, product(): jnp.dot(left_side, right_side, precision=highest, preferred_element_type=...  17.8 us
    select_n x1, other arithmetic, on_device(): jnp.where(live_all[:, :, None, None], jnp.take(flat_local, pick_all * 2 +...  5.11 us
    all_to_all x1, starting transfers between devices, on_device(): lax.all_to_all(outgoing, 'shard', split_axis=0, concat_axis=0, tiled=True)  4.62 us
  transfers between devices with their start and end apart: 4, of which 3 were waited for; matrix products, arithmetic and copies ran while one was open for 4% of the time, Pallas kernels for 0%

commit v1 on v0

--- a/solution.py
+++ b/solution.py
@@ -1,6 +1,10 @@
+import functools
+
 import jax
 import jax.numpy as jnp
 from jax import lax
+from jax.experimental import pallas as pl
+from jax.experimental.pallas import tpu as pltpu
 from jax.sharding import PartitionSpec as P
 
 B = 512
@@ -47,6 +51,13 @@
     )
 
 
+def pick(array, index):
+    flat = lax.map(
+        lambda i: lax.dynamic_index_in_dim(array, i, 0, keepdims=False), index.reshape(-1)
+    )
+    return flat.reshape(index.shape + array.shape[1:])
+
+
 def on_device(stats_partial, gradient, owner_of, layer_count):
     shards = lax.axis_size("shard")
     groups = lax.axis_size("dp")
@@ -70,7 +81,10 @@
     )
     grad_pick = jnp.take(chosen, all_places)
     grad_live = jnp.take(filled, all_places)
-    layer_ends = jnp.cumsum(layer_count)
+    layer_ids = jnp.arange(LAYERS)
+    layer_ends = jnp.sum(
+        jnp.where(layer_ids[:, None] <= layer_ids[None, :], layer_count[:, None], 0), axis=0
+    )
     layer_of = jnp.sum((block_ids[:, None] >= layer_ends[None, :]).astype(jnp.int32), axis=1)
     local = stats_partial[0]
     local_rows = local.shape[2]
@@ -82,7 +96,7 @@
     flat_local = local.reshape(blocks * 2, local_rows, B)
     laid = jnp.where(
         live_all[:, :, None, None],
-        jnp.take(flat_local, pick_all * 2 + (members % 2)[:, None], axis=0),
+        pick(flat_local, pick_all * 2 + (members % 2)[:, None]),
         0.0,
     )
     outgoing = lax.psum_scatter(laid, "dp", scatter_dimension=0, tiled=True)[0]
@@ -95,7 +109,7 @@
     factors = lax.all_gather(factor[None], "dp", axis=0, tiled=True).reshape(OCAP, 2, B, B)
     grad_send = jnp.where(
         grad_live[:, :, None, None],
-        jnp.take(gradient, grad_pick, axis=0),
+        pick(gradient, grad_pick),
         jnp.zeros((), jnp.bfloat16),
     )
     grad_full = lax.all_to_all(grad_send, "shard", split_axis=1, concat_axis=1, tiled=True).reshape(
@@ -121,10 +135,300 @@
     return scaled[None]
 
 
+MESH = pl.DeviceIdType.MESH
+
+
+def root_of(total):
+    n = total.shape[0]
+
+    def times(a, b):
+        return jnp.dot(
+            a.astype(jnp.bfloat16), b.astype(jnp.bfloat16), preferred_element_type=jnp.float32
+        )
+
+    mean_square = jnp.sum(total * total, axis=(0, 1), keepdims=True) * (1.0 / (n * n))
+    magnitude = n * jnp.sqrt(mean_square + 1e-06)
+    scale = 1.0 / jnp.sqrt(jnp.sqrt(magnitude))
+
+    def next_matrix(quarter):
+        w = 2.5 * quarter - times(quarter, quarter)
+        v = 3.125 * w - times(w, w)
+        return 2.44140625 * quarter - times(v, quarter)
+
+    first = total * (0.25 / magnitude)
+    second = next_matrix(first)
+    both = 1.25 * (first + second) - times(first, second)
+    third = next_matrix(second)
+    rest = 1.25 * both + 1.5625 * third - times(both, third)
+    rows = lax.broadcasted_iota(jnp.int32, (n, n), 0)
+    columns = lax.broadcasted_iota(jnp.int32, (n, n), 1)
+    return ((jnp.where(rows == columns, 1.953125, 0.0) - rest) * scale).astype(jnp.bfloat16)
+
+
+def refresh(
+    shards, stats, grad, owner, counts, out,
+    xs, xr, ys, yr, keep, zs, whole, gcols, factor, mid, midr, raw, gath, vec, vecr, vecs, vecz,
+    x_sem, y_sem, z_sem, g_sem, h_sem, m_sem, r_sem, a_sem, f_sem, n_sem, o_sem, l_sem,
+):
+    s = lax.axis_index("shard")
+    m = lax.axis_index("dp")
+    x, y = lax.rem(m, 2), m // 2
+    blocks, _, rows, n = stats.shape
+    half, quarter = n // 2, n // 4
+    x_peer, y_peer = y * 2 + 1 - x, (1 - y) * 2 + x
+    diagonal = (1 - y) * 2 + 1 - x
+
+    barrier = pltpu.get_barrier_semaphore()
+    for d in (x_peer, y_peer, diagonal):
+        pl.semaphore_signal(barrier, inc=1, device_id=(d, s), device_id_type=MESH)
+    for k in range(1, shards):
+        pl.semaphore_signal(
+            barrier, inc=1, device_id=(m, lax.rem(s + k, shards)), device_id_type=MESH
+        )
+
+    def remote(source, target, sems, i, device):
+        return pltpu.make_async_remote_copy(
+            src_ref=source, dst_ref=target, send_sem=sems.at[0, i], recv_sem=sems.at[1, i],
+            device_id=device, device_id_type=MESH,
+        )
+
+    def columns(which):
+        return pl.ds(pl.multiple_of(which * half, half), half)
+
+    def own_rows(which):
+        return pl.ds(pl.multiple_of(which * rows, rows), rows)
+
+    order = [lax.rem(s + k, shards) for k in range(shards)]
+    for k in range(blocks):
+        xs[k] = stats[order[k], 1 - x].astype(jnp.bfloat16)
+    pl.semaphore_wait(barrier, shards + 2)
+
+    x_copies, y_copies, z_copies, g_copies = [], [], [], []
+    for k in range(blocks):
+        c = remote(xs.at[k], xr.at[k], x_sem, k, (x_peer, s))
+        c.start()
+        x_copies.append(c)
+    for k in range(1, shards):
+        c = remote(
+            grad.at[order[k], :, columns(y)], gcols.at[own_rows(s)], g_sem, k, (m, order[k])
+        )
+        c.start()
+        g_copies.append(c)
+    local = pltpu.make_async_copy(
+        grad.at[s, :, columns(y)], gcols.at[own_rows(s)], l_sem.at[0]
+    )
+    local.start()
+    lanes = lax.broadcasted_iota(jnp.int32, (8, 128), 1)
+    lane_row = lax.broadcasted_iota(jnp.int32, (8, 128), 0)
+    squares = jnp.zeros((8, 128), jnp.float32)
+    for b in range(blocks):
+        g = grad[b].astype(jnp.float32)
+        squares = jnp.where(
+            (lane_row == 1) & (lanes == b),
+            jnp.sum(g * g, axis=(0, 1), keepdims=True) * 0.25,
+            squares,
+        )
+    for t in range(blocks + 2):
+        if t < blocks:
+            x_copies[t].wait_recv()
+            mine = stats[order[t], x] + xr[t].astype(jnp.float32)
+            left, right = mine[:, :half], mine[:, half:]
+            keep[t] = jnp.where(y == 0, left, right)
+            ys[t] = jnp.where(y == 0, right, left).astype(jnp.bfloat16)
+            c = remote(ys.at[t], yr.at[t], y_sem, t, (y_peer, s))
+            c.start()
+            y_copies.append(c)
+        if t >= 2:
+            k = t - 2
+            y_copies[k].wait_recv()
+            zs[k] = (keep[k] + yr[k].astype(jnp.float32)).astype(jnp.bfloat16)
+            if k > 0:
+                c = remote(zs.at[k], whole.at[y, own_rows(s)], z_sem, k, (m, order[k]))
+                c.start()
+                z_copies.append(c)
+    own = pltpu.make_async_copy(zs.at[0], whole.at[y, own_rows(s)], l_sem.at[1])
+    own.start()
+    own.wait()
+    for c in z_copies:
+        c.wait_recv()
+    h_copy = remote(whole.at[y], whole.at[y], h_sem, 0, (y_peer, s))
+    h_copy.start()
+    h_copy.wait_recv()
+    factor[...] = root_of(
+        jnp.concatenate([whole[0], whole[1]], axis=1).astype(jnp.float32)
+    )
+    local.wait()
+    for c in g_copies:
+        c.wait_recv()
+
+    piece = pl.ds(0, quarter)
+    other = remote(raw.at[piece], gath.at[s], r_sem, 0, (x_peer, s))
+
+    @pl.when(x == 0)
+    def _():
+        mid[...] = jnp.dot(
+            factor[...], gcols[...], preferred_element_type=jnp.float32
+        ).astype(jnp.bfloat16)
+        a = remote(mid.at[columns(y)], midr.at[y], m_sem, 0, (x_peer, s))
+        b = remote(mid.at[columns(1 - y)], midr.at[y], m_sem, 1, (diagonal, s))
+        b.start()
+        a.start()
+        vec[...] = squares
+        a.wait_send()
+        b.wait_send()
+        other.wait_recv()
+
+    @pl.when(x == 1)
+    def _():
+        a = remote(mid.at[columns(y)], midr.at[y], m_sem, 0, (x_peer, s))
+        b = remote(mid.at[columns(1 - y)], midr.at[1 - y], m_sem, 1, (diagonal, s))
+        a.wait_recv()
+        b.wait_recv()
+        result = jnp.dot(midr[0], factor[:half], preferred_element_type=jnp.float32) + jnp.dot(
+            midr[1], factor[half:], preferred_element_type=jnp.float32
+        )
+        raw[...] = result.astype(jnp.bfloat16)
+        other.start()
+        gath[s] = raw[quarter:]
+        vec[...] = jnp.where(
+            (lane_row == 0) & (lanes == s),
+            jnp.sum(result * result, axis=(0, 1), keepdims=True),
+            squares,
+        )
+        other.wait_send()
+
+    neighbour = s + 1 - 2 * lax.rem(s, 2)
+    far, near = [], []
+    for k in range(1, shards // 2):
+        c = remote(gath.at[s], gath.at[s], a_sem, k, (m, order[2 * k]))
+        c.start()
+        far.append(c)
+    c = remote(gath.at[s], gath.at[s], f_sem, 0, (m, neighbour))
+    c.start()
+    near.append(c)
+    norms = []
+    for i, d in enumerate((x_peer, y_peer, diagonal)):
+        c = remote(vec, vecr.at[i], n_sem, i, (d, s))
+        c.start()
+        norms.append(c)
+    for c in norms:
+        c.wait_recv()
+    vecs[...] = vec[...] + vecr[0] + vecr[1] + vecr[2]
+    for k in range(1, shards):
+        c = remote(vecs, vecz.at[k - 1], o_sem, k, (m, order[k]))
+        c.start()
+        norms.append(c)
+
+    for k in range(1, shards // 2):
+        far[k - 1].wait_recv()
+        origin = lax.rem(s + shards - 2 * k, shards)
+        c = remote(gath.at[origin], gath.at[origin], f_sem, k, (m, neighbour))
+        c.start()
+        near.append(c)
+    for c in norms[3:]:
+        c.wait_recv()
+    totals = vecs[...] + jnp.sum(vecz[...], axis=0)
+    raw_sq, grad_sq = totals[0:1], totals[1:2]
+
+    ends, layer = [], []
+    for l in range(counts.shape[0]):
+        ends.append(counts[l] + (ends[-1] if ends else 0))
+    for b in range(blocks):
+        layer.append(sum(jnp.where(b >= e, 1, 0) for e in ends))
+    count = jnp.int32(0)
+    chosen = [jnp.int32(0)] * OCAP
+    chosen_layer = [jnp.int32(-1)] * OCAP
+    for b in range(blocks):
+        is_mine = owner[b] == s
+        for k in range(OCAP):
+            hit = is_mine & (count == k)
+            chosen[k] = jnp.where(hit, b, chosen[k])
+            chosen_layer[k] = jnp.where(hit, layer[b], chosen_layer[k])
+        count = count + jnp.where(is_mine, 1, 0)
+    lane = lax.broadcasted_iota(jnp.int32, (1, 128), 1)
+    layer_lane = jnp.full((1, 128), -2, jnp.int32)
+    for b in range(blocks):
+        layer_lane = jnp.where(lane == b, layer[b], layer_lane)
+    scales = []
+    for k in range(OCAP):
+        same = layer_lane == chosen_layer[k]
+        top = jnp.sum(jnp.where(same, grad_sq, 0.0), axis=1, keepdims=True)
+        bottom = jnp.sum(jnp.where(same, raw_sq, 0.0), axis=1, keepdims=True)
+        live = jnp.where(count > k, 1.0, 0.0)
+        scales.append(live * jnp.sqrt((top + 1e-06) / (bottom + 1e-06)))
+
+    for c in near:
+        c.wait_recv()
+    for k in range(OCAP):
+        out[k] = (gath[chosen[k]].astype(jnp.float32) * scales[k]).astype(jnp.bfloat16)
+    for c in x_copies + y_copies + z_copies + g_copies + [h_copy] + far + near + norms:
+        c.wait_send()
+
+
+def refreshed(stats_partial, gradient, owner_of, layer_count):
+    shards = lax.axis_size("shard")
+    stats = stats_partial[0]
+    blocks, _, rows, n = stats.shape
+    half, quarter = n // 2, n // 4
+    bf16, f32 = jnp.bfloat16, jnp.float32
+    vmem = pltpu.VMEM
+    sems = lambda count: pltpu.SemaphoreType.DMA((2, count))
+    out = pl.pallas_call(
+        functools.partial(refresh, shards),
+        out_shape=jax.ShapeDtypeStruct((OCAP, quarter, n), bf16),
+        in_specs=[pl.BlockSpec(memory_space=pltpu.VMEM)] * 2
+        + [pl.BlockSpec(memory_space=pltpu.SMEM)] * 2,
+        out_specs=pl.BlockSpec(memory_space=pltpu.VMEM),
+        scratch_shapes=[
+            vmem((blocks, rows, n), bf16),
+            vmem((blocks, rows, n), bf16),
+            vmem((blocks, rows, half), bf16),
+            vmem((blocks, rows, half), bf16),
+            vmem((blocks, rows, half), f32),
+            vmem((blocks, rows, half), bf16),
+            vmem((2, n, half), bf16),
+            vmem((n, half), bf16),
+            vmem((n, n), bf16),
+            vmem((n, half), bf16),
+            vmem((2, half, half), bf16),
+            vmem((half, n), bf16),
+            vmem((blocks, quarter, n), bf16),
+            vmem((8, 128), f32),
+            vmem((3, 8, 128), f32),
+            vmem((8, 128), f32),
+            vmem((shards - 1, 8, 128), f32),
+            sems(blocks),
+            sems(blocks),
+            sems(blocks),
+            sems(shards),
+            sems(1),
+            sems(2),
+            sems(1),
+            sems(shards // 2),
+            sems(shards // 2),
+            sems(3),
+            sems(shards),
+            pltpu.SemaphoreType.DMA((2,)),
+        ],
+        compiler_params=pltpu.CompilerParams(
+            collective_id=0, has_side_effects=True, vmem_limit_bytes=48 * 2**20
+        ),
+    )(stats, gradient, owner_of, layer_count)
+    return out[None]
+
+
 def solution(mesh):
     placed = (P("dp", None, None, "shard", None), P(None, "shard", None), P(), P())
+    groups, shards = mesh.shape["dp"], mesh.shape["shard"]
+
+    def program(stats_partial, gradient, owner_of, layer_count):
+        blocks, strip = owner_of.shape[0], stats_partial.shape[3]
+        fits = (groups, blocks) == (4, shards) and shards % 2 == 0 and strip % 16 == 0
+        body = refreshed if fits and blocks <= 128 else on_device
+        return body(stats_partial, gradient, owner_of, layer_count)
+
     return jax.shard_map(
-        on_device,
+        program,
         mesh=mesh,
         in_specs=placed,
         out_specs=P("shard", None, "dp", None),

time: 214 us -> 65.9 us (0.31)
  waiting for transfers between devices: 106 us -> 0 us
  Pallas kernels: 0 us -> 61 us
  blocking collectives: 36.9 us -> 0 us
  matrix products: 20.4 us -> 0 us
  between operations: 15.1 us -> 0.01 us
  other arithmetic: 11.7 us -> 0 us
  local copies, waits for them, and re-layouts: 14.6 us -> 4.65 us
  starting transfers between devices: 8.9 us -> 0 us
    pallas_call x0 -> x1, Pallas kernels: none -> 61 us  [refreshed(): pl.pallas_call(functools.partial(refresh, shards), out_shape=jax.ShapeDty...]
    unnamed x3 -> x0, waiting for transfers between devices: 55.6 us -> none
    all_to_all x2 -> x0, waiting for transfers between devices: 50.1 us -> none  [the longest x1 25.2 us: on_device(): lax.all_to_all(outgoing, 'shard', split_axis=0, concat_axis=0, tiled=True)]
    psum x1 -> x0, blocking collectives: 36.9 us -> none  [on_device(): lax.psum((jnp.sum(layer_hot * grad_terms[:, None], axis=0), jnp.sum(layer...]
    dot_general x10 -> x0, matrix products: 20.4 us -> none  [the longest x9 17.8 us: product(): jnp.dot(left_side, right_side, precision=highest, preferred_element_type=...]
    gather x14 -> x0, local copies, waits for them, and re-layouts: 8.98 us -> none  [the longest x1 2.8 us: on_device(): jnp.take(flat_local, pick_all * 2 + (members % 2)[:, None], axis=0)]
    all_to_all x2 -> x0, starting transfers between devices: 8.86 us -> none  [the longest x1 4.62 us: on_device(): lax.all_to_all(outgoing, 'shard', split_axis=0, concat_axis=0, tiled=True)]
    select_n x12 -> x0, other arithmetic: 5.62 us -> none  [the longest x1 5.11 us: on_device(): jnp.where(live_all[:, :, None, None], jnp.take(flat_local, pick_all * 2 +...]
  transfers between devices with their start and end apart: 4 -> 0, of which waited for: 3 -> 0; matrix products, arithmetic and copies ran while one was open for 4% -> 0% of each run, Pallas kernels for 0% -> 0%
where the time goes in v1:
time: 65.9 us; the launch traced here: 65.7 us
  Pallas kernels  61 us (93%)
  local copies, waits for them, and re-layouts  4.65 us (7%)
    pallas_call x1, Pallas kernels, refreshed(): pl.pallas_call(functools.partial(refresh, shards), out_shape=jax.ShapeDty...  61 us
    unnamed x9, local copies, waits for them, and re-layouts  4.65 us

profile of v1, /device:TPU:0, one launch (start us, length us, event | category | flops | bytes accessed | tf_op | source)
XLA Modules:
  0.0 65.7 jit_solution(15747272606102882808)
XLA Ops:
  0.0 0.0 copy-start
  0.0 1.6 %copy-done = f32[1,8,2,64,512]{4,3,2,1,0:T(8,128)S(1)} copy-done((f32[1,8,2,64,512]{4,3,2,1,0:T(8,128)S(1)}, f32[1,8,2,64,512]{4,3,2,1,0:T(8,128)}, u32[]{:S(2)}) %copy-start) | copy-done | bytes 2097176
  1.6 0.0 copy-start.1
  1.6 1.0 %copy-done.1 = bf16[8,64,512]{2,1,0:T(8,128)(2,1)S(1)} copy-done((bf16[8,64,512]{2,1,0:T(8,128)(2,1)S(1)}, bf16[8,64,512]{2,1,0:T(8,128)(2,1)}, u32[]{:S(2)}) %copy-start.1) | copy-done | bytes 524312
  2.6 0.0 copy-start.2
  2.6 0.7 copy-done.2
  3.3 0.0 copy-start.3
  3.3 0.7 copy-done.3
  3.9 61.0 %shard_map.46 = bf16[2,128,512]{2,1,0:T(8,128)(2,1)S(1)} custom-call(f32[8,2,64,512]{3,2,1,0:T(8,128)S(1)} %bitcast.2, bf16[8,64,512]{2,1,0:T(8,128)(2,1)S(1)} %copy-done.1, s32[8]{0:T(128)S(1)} %copy-done.2, s32[4]{0:T(128)S(1)} %copy-done.3), custom_call_target="tpu_custom_call" | custom-call | tf_op jit(solution)/shard_map/pallas_call | solution.py:376
  65.0 0.7 %copy.6 = bf16[1,2,128,512]{3,2,1,0:T(8,128)(2,1)} copy(bf16[1,2,128,512]{3,2,1,0:T(8,128)(2,1)S(1)} %bitcast.3) | data formatting | bytes 524288
Async XLA Ops:
  0.0 1.6 %copy-start = (f32[1,8,2,64,512]{4,3,2,1,0:T(8,128)S(1)}, f32[1,8,2,64,512]{4,3,2,1,0:T(8,128)}, u32[]{:S(2)}) copy-start(f32[1,8,2,64,512]{4,3,2,1,0:T(8,128)} %param.4) | copy-start | bytes 6291460
  1.6 1.0 %copy-start.1 = (bf16[8,64,512]{2,1,0:T(8,128)(2,1)S(1)}, bf16[8,64,512]{2,1,0:T(8,128)(2,1)}, u32[]{:S(2)}) copy-start(bf16[8,64,512]{2,1,0:T(8,128)(2,1)} %grad.1) | copy-start | bytes 1572868
  2.6 0.7 copy-start.2
  3.3 0.7 copy-start.3

commit v2 on v1

--- a/solution.py
+++ b/solution.py
@@ -136,6 +136,7 @@
 
 
 MESH = pl.DeviceIdType.MESH
+PIECES = 2
 
 
 def root_of(total):
@@ -166,18 +167,33 @@
 
 
 def refresh(
-    shards, stats, grad, owner, counts, out,
+    shards, stats_in, grad_in, owner_in, counts_in, out, theirs, ours, grad, owner, counts,
     xs, xr, ys, yr, keep, zs, whole, gcols, factor, mid, midr, raw, gath, vec, vecr, vecs, vecz,
     x_sem, y_sem, z_sem, g_sem, h_sem, m_sem, r_sem, a_sem, f_sem, n_sem, o_sem, l_sem,
 ):
     s = lax.axis_index("shard")
     m = lax.axis_index("dp")
     x, y = lax.rem(m, 2), m // 2
-    blocks, _, rows, n = stats.shape
+    blocks, rows, n = theirs.shape
     half, quarter = n // 2, n // 4
+    piece = quarter // PIECES
     x_peer, y_peer = y * 2 + 1 - x, (1 - y) * 2 + x
     diagonal = (1 - y) * 2 + 1 - x
 
+    loads = [
+        pltpu.make_async_copy(source, target, l_sem.at[i])
+        for i, (source, target) in enumerate(
+            (
+                (stats_in.at[:, 1 - x], theirs),
+                (stats_in.at[:, x], ours),
+                (grad_in, grad),
+                (owner_in, owner),
+                (counts_in, counts),
+            )
+        )
+    ]
+    for c in loads:
+        c.start()
     barrier = pltpu.get_barrier_semaphore()
     for d in (x_peer, y_peer, diagonal):
         pl.semaphore_signal(barrier, inc=1, device_id=(d, s), device_id_type=MESH)
@@ -199,8 +215,9 @@
         return pl.ds(pl.multiple_of(which * rows, rows), rows)
 
     order = [lax.rem(s + k, shards) for k in range(shards)]
+    loads[0].wait()
     for k in range(blocks):
-        xs[k] = stats[order[k], 1 - x].astype(jnp.bfloat16)
+        xs[k] = theirs[order[k]].astype(jnp.bfloat16)
     pl.semaphore_wait(barrier, shards + 2)
 
     x_copies, y_copies, z_copies, g_copies = [], [], [], []
@@ -208,6 +225,8 @@
         c = remote(xs.at[k], xr.at[k], x_sem, k, (x_peer, s))
         c.start()
         x_copies.append(c)
+    loads[1].wait()
+    loads[2].wait()
     for k in range(1, shards):
         c = remote(
             grad.at[order[k], :, columns(y)], gcols.at[own_rows(s)], g_sem, k, (m, order[k])
@@ -215,7 +234,7 @@
         c.start()
         g_copies.append(c)
     local = pltpu.make_async_copy(
-        grad.at[s, :, columns(y)], gcols.at[own_rows(s)], l_sem.at[0]
+        grad.at[s, :, columns(y)], gcols.at[own_rows(s)], l_sem.at[5]
     )
     local.start()
     lanes = lax.broadcasted_iota(jnp.int32, (8, 128), 1)
@@ -231,7 +250,7 @@
     for t in range(blocks + 2):
         if t < blocks:
             x_copies[t].wait_recv()
-            mine = stats[order[t], x] + xr[t].astype(jnp.float32)
+            mine = ours[order[t]] + xr[t].astype(jnp.float32)
             left, right = mine[:, :half], mine[:, half:]
             keep[t] = jnp.where(y == 0, left, right)
             ys[t] = jnp.where(y == 0, right, left).astype(jnp.bfloat16)
@@ -246,14 +265,19 @@
                 c = remote(zs.at[k], whole.at[y, own_rows(s)], z_sem, k, (m, order[k]))
                 c.start()
                 z_copies.append(c)
-    own = pltpu.make_async_copy(zs.at[0], whole.at[y, own_rows(s)], l_sem.at[1])
+    own = pltpu.make_async_copy(zs.at[0], whole.at[y, own_rows(s)], l_sem.at[6])
     own.start()
     own.wait()
-    for c in z_copies:
+    h_copies = []
+    for k in range(blocks):
+        if k > 0:
+            z_copies[k - 1].wait_recv()
+        at = whole.at[y, own_rows(lax.rem(s + shards - k, shards))]
+        c = remote(at, at, h_sem, k, (y_peer, s))
+        c.start()
+        h_copies.append(c)
+    for c in h_copies:
         c.wait_recv()
-    h_copy = remote(whole.at[y], whole.at[y], h_sem, 0, (y_peer, s))
-    h_copy.start()
-    h_copy.wait_recv()
     factor[...] = root_of(
         jnp.concatenate([whole[0], whole[1]], axis=1).astype(jnp.float32)
     )
@@ -261,56 +285,76 @@
     for c in g_copies:
         c.wait_recv()
 
-    piece = pl.ds(0, quarter)
-    other = remote(raw.at[piece], gath.at[s], r_sem, 0, (x_peer, s))
+    levels = shards // 2
+    neighbour = s + 1 - 2 * lax.rem(s, 2)
+
+    def part(i):
+        return pl.ds(i * piece, piece)
+
+    def across(i):
+        return remote(raw.at[part(i)], gath.at[s, part(i)], r_sem, i, (x_peer, s))
+
+    def along(k, i):
+        at = gath.at[s, part(i)]
+        return remote(at, at, a_sem, k * PIECES + i, (m, order[2 * k]))
+
+    def sideways(k, i):
+        at = gath.at[lax.rem(s + shards - 2 * k, shards), part(i)]
+        return remote(at, at, f_sem, k * PIECES + i, (m, neighbour))
+
+    def spread(i):
+        for k in range(1, levels):
+            along(k, i).start()
+        sideways(0, i).start()
+
+    turns = [i + q * PIECES for q in (0, 1) for i in range(PIECES)]
 
     @pl.when(x == 0)
     def _():
-        mid[...] = jnp.dot(
-            factor[...], gcols[...], preferred_element_type=jnp.float32
-        ).astype(jnp.bfloat16)
-        a = remote(mid.at[columns(y)], midr.at[y], m_sem, 0, (x_peer, s))
-        b = remote(mid.at[columns(1 - y)], midr.at[y], m_sem, 1, (diagonal, s))
-        b.start()
-        a.start()
+        sent = []
+        for t in turns:
+            for slot, (to, d) in enumerate(((1 - y, diagonal), (y, x_peer))):
+                at = pl.ds(pl.multiple_of(to * half + t * piece, piece), piece)
+                mid[at] = jnp.dot(
+                    factor[at], gcols[...], preferred_element_type=jnp.float32
+                ).astype(jnp.bfloat16)
+                c = remote(mid.at[at], midr.at[y, part(t)], m_sem, 2 * t + slot, (d, s))
+                c.start()
+                sent.append(c)
         vec[...] = squares
-        a.wait_send()
-        b.wait_send()
-        other.wait_recv()
+        for i in range(PIECES):
+            across(i).wait_recv()
+            spread(i)
+        for c in sent:
+            c.wait_send()
 
     @pl.when(x == 1)
     def _():
-        a = remote(mid.at[columns(y)], midr.at[y], m_sem, 0, (x_peer, s))
-        b = remote(mid.at[columns(1 - y)], midr.at[1 - y], m_sem, 1, (diagonal, s))
-        a.wait_recv()
-        b.wait_recv()
-        result = jnp.dot(midr[0], factor[:half], preferred_element_type=jnp.float32) + jnp.dot(
-            midr[1], factor[half:], preferred_element_type=jnp.float32
-        )
-        raw[...] = result.astype(jnp.bfloat16)
-        other.start()
-        gath[s] = raw[quarter:]
-        vec[...] = jnp.where(
-            (lane_row == 0) & (lanes == s),
-            jnp.sum(result * result, axis=(0, 1), keepdims=True),
-            squares,
-        )
-        other.wait_send()
-
-    neighbour = s + 1 - 2 * lax.rem(s, 2)
-    far, near = [], []
-    for k in range(1, shards // 2):
-        c = remote(gath.at[s], gath.at[s], a_sem, k, (m, order[2 * k]))
-        c.start()
-        far.append(c)
-    c = remote(gath.at[s], gath.at[s], f_sem, 0, (m, neighbour))
-    c.start()
-    near.append(c)
+        total = jnp.zeros((1, 1), jnp.float32)
+        for t in turns:
+            for slot, (source, d) in enumerate(((1 - y, diagonal), (y, x_peer))):
+                at = midr.at[source, part(t)]
+                remote(at, at, m_sem, 2 * t + slot, (d, s)).wait_recv()
+            result = jnp.dot(
+                midr[0, part(t)], factor[:half], preferred_element_type=jnp.float32
+            ) + jnp.dot(midr[1, part(t)], factor[half:], preferred_element_type=jnp.float32)
+            if t < PIECES:
+                raw[part(t)] = result.astype(jnp.bfloat16)
+                across(t).start()
+            else:
+                gath[s, part(t - PIECES)] = result.astype(jnp.bfloat16)
+                spread(t - PIECES)
+            total = total + jnp.sum(result * result, axis=(0, 1), keepdims=True)
+        vec[...] = jnp.where((lane_row == 0) & (lanes == s), total, squares)
+        for i in range(PIECES):
+            across(i).wait_send()
+
     norms = []
     for i, d in enumerate((x_peer, y_peer, diagonal)):
         c = remote(vec, vecr.at[i], n_sem, i, (d, s))
         c.start()
         norms.append(c)
+
     for c in norms:
         c.wait_recv()
     vecs[...] = vec[...] + vecr[0] + vecr[1] + vecr[2]
@@ -318,15 +362,14 @@
         c = remote(vecs, vecz.at[k - 1], o_sem, k, (m, order[k]))
         c.start()
         norms.append(c)
-
-    for k in range(1, shards // 2):
-        far[k - 1].wait_recv()
-        origin = lax.rem(s + shards - 2 * k, shards)
-        c = remote(gath.at[origin], gath.at[origin], f_sem, k, (m, neighbour))
-        c.start()
-        near.append(c)
+    for i in range(PIECES):
+        for k in range(1, levels):
+            along(k, i).wait_recv()
+            sideways(k, i).start()
     for c in norms[3:]:
         c.wait_recv()
+    loads[3].wait()
+    loads[4].wait()
     totals = vecs[...] + jnp.sum(vecz[...], axis=0)
     raw_sq, grad_sq = totals[0:1], totals[1:2]
 
@@ -357,12 +400,18 @@
         live = jnp.where(count > k, 1.0, 0.0)
         scales.append(live * jnp.sqrt((top + 1e-06) / (bottom + 1e-06)))
 
-    for c in near:
-        c.wait_recv()
+    for i in range(PIECES):
+        for k in range(levels):
+            sideways(k, i).wait_recv()
     for k in range(OCAP):
         out[k] = (gath[chosen[k]].astype(jnp.float32) * scales[k]).astype(jnp.bfloat16)
-    for c in x_copies + y_copies + z_copies + g_copies + [h_copy] + far + near + norms:
+    for c in x_copies + y_copies + z_copies + g_copies + h_copies + norms:
         c.wait_send()
+    for i in range(PIECES):
+        for k in range(levels):
+            sideways(k, i).wait_send()
+            if k:
+                along(k, i).wait_send()
 
 
 def refreshed(stats_partial, gradient, owner_of, layer_count):
@@ -376,10 +425,14 @@
     out = pl.pallas_call(
         functools.partial(refresh, shards),
         out_shape=jax.ShapeDtypeStruct((OCAP, quarter, n), bf16),
-        in_specs=[pl.BlockSpec(memory_space=pltpu.VMEM)] * 2
-        + [pl.BlockSpec(memory_space=pltpu.SMEM)] * 2,
+        in_specs=[pl.BlockSpec(memory_space=pltpu.HBM)] * 4,
         out_specs=pl.BlockSpec(memory_space=pltpu.VMEM),
         scratch_shapes=[
+            vmem((blocks, rows, n), f32),
+            vmem((blocks, rows, n), f32),
+            vmem((blocks, rows, n), bf16),
+            pltpu.SMEM(owner_of.shape, jnp.int32),
+            pltpu.SMEM(layer_count.shape, jnp.int32),
             vmem((blocks, rows, n), bf16),
             vmem((blocks, rows, n), bf16),
             vmem((blocks, rows, half), bf16),
@@ -391,7 +444,7 @@
             vmem((n, n), bf16),
             vmem((n, half), bf16),
             vmem((2, half, half), bf16),
-            vmem((half, n), bf16),
+            vmem((quarter, n), bf16),
             vmem((blocks, quarter, n), bf16),
             vmem((8, 128), f32),
             vmem((3, 8, 128), f32),
@@ -401,17 +454,17 @@
             sems(blocks),
             sems(blocks),
             sems(shards),
-            sems(1),
-            sems(2),
-            sems(1),
-            sems(shards // 2),
-            sems(shards // 2),
+            sems(blocks),
+            sems(4 * PIECES),
+            sems(PIECES),
+            sems(shards // 2 * PIECES),
+            sems(shards // 2 * PIECES),
             sems(3),
             sems(shards),
-            pltpu.SemaphoreType.DMA((2,)),
+            pltpu.SemaphoreType.DMA((7,)),
         ],
         compiler_params=pltpu.CompilerParams(
-            collective_id=0, has_side_effects=True, vmem_limit_bytes=48 * 2**20
+            collective_id=0, has_side_effects=True, vmem_limit_bytes=62 * 2**20
         ),
     )(stats, gradient, owner_of, layer_count)
     return out[None]

time: 65.9 us -> 54.2 us (0.82)
  Pallas kernels: 61 us -> 52.4 us
  local copies, waits for them, and re-layouts: 4.65 us -> 1.67 us
    pallas_call x1, Pallas kernels: 61 us -> 52.4 us  [refreshed(): pl.pallas_call(functools.partial(refresh, shards), out_shape=jax.ShapeDty...]
    unnamed x9 -> x1, local copies, waits for them, and re-layouts: 4.65 us -> 1.67 us
where the time goes in v2:
time: 54.2 us; the launch traced here: 54.1 us
  Pallas kernels  52.4 us (97%)
  local copies, waits for them, and re-layouts  1.67 us (3%)
    pallas_call x1, Pallas kernels, refreshed(): pl.pallas_call(functools.partial(refresh, shards), out_shape=jax.ShapeDty...  52.4 us
    unnamed x1, local copies, waits for them, and re-layouts  1.67 us

profile of v2, /device:TPU:0, one launch (start us, length us, event | category | flops | bytes accessed | tf_op | source)
XLA Modules:
  0.0 54.1 jit_solution(17123816123017434135)
XLA Ops:
  0.0 52.4 %shard_map.46 = bf16[2,128,512]{2,1,0:T(8,128)(2,1)} custom-call(f32[8,2,64,512]{3,2,1,0:T(8,128)} %bitcast.2, bf16[8,64,512]{2,1,0:T(8,128)(2,1)} %grad_in.1, s32[8]{0:T(128)} %owner_in.1, s32[4]{0:T(128)} %counts_in.1), custom_call_target="tpu_custom_call" | custom-call | tf_op jit(solution)/shard_map/pallas_call | solution.py:425
  52.4 1.7 %copy.6 = bf16[1,2,128,512]{3,2,1,0:T(8,128)(2,1)} copy(bf16[1,2,128,512]{3,2,1,0:T(8,128)(2,1)} %bitcast.3) | data formatting | bytes 524288
